TPU v7x, 128 devices: a whole 4x4x4 slice. The times are simulated.
128 devices in a mesh: ty: 8 (over x, core), tx: 16 (over z, y).
Axes of the slice: x: 4, y: 4, z: 4, core: 2. Of those that a mesh axis runs over, the one named last changes fastest.
Arguments:
- beam_depth: float32 [8192, 512], P(('ty', 'tx')), may hold values from -6 to 6
- backscatter: float32 [8192, 512], P(('ty', 'tx')), may hold values from -6 to 6
- grazing: float32 [8192, 512], P(('ty', 'tx')), may hold values from -6 to 6
- quality: float32 [8192, 512], P(('ty', 'tx')), may hold values from 0.25 to 2
- beam_valid: int32 [8192, 512], P(('ty', 'tx')), may hold values 0 or 1
- beam_row: int32 [8192, 512], P(('ty', 'tx')), may hold values from 0 to 63
- beam_col: int32 [8192, 512], P(('ty', 'tx')), may hold values from 0 to 63
- tidal_zone: int32 [8192], P(('ty', 'tx')), may hold values from 0 to 63
- ping_tile: int32 [8192], P(('ty', 'tx')), may hold values from 0 to 127, as said below
- tide_offsets: float32 [64], replicated, may hold values from -1 to 1
Outputs:
- gridded: float32 [8, 512, 1024], P(None, 'ty', 'tx')
Inputs may be any that keep to these rules, and one draw needn't show every extreme that they name: `ping_tile`: tile t is the tile in row t // 16 and column t % 16. In each aligned block of 64 pings no tile is named more than 2 times, and one tile is named exactly 2 times in every block.
All inputs are finite; a program needn't handle non-finite values. No bound on the sum of `beam_valid` on one device may be relied on, other than what follows from the above.
Results may differ from a plain program's by a relative error of at most 0.000073.
Values sent between devices are 32-bit elements; how exact they have to be, the bound alone decides.
No kernel may reach another device: no remote copies, remote signals or barrier semaphores. Data moves between devices by JAX's collectives and lax.ppermute only.
A program may use at most 64 MiB of HBM per device.

v0:
```python
import math

import jax
import jax.numpy as jnp
from jax import lax
from jax.sharding import PartitionSpec as P

MARGIN = 7
TILE = 64


gauss_sigma = 2.5


def extended_2(cells, sides, width):
    for axis, dim in sides:
        count = lax.axis_size(axis)
        ends = count - 1
        head = lax.slice_in_dim(cells, 0, width, axis=dim)
        tail = lax.slice_in_dim(cells, cells.shape[dim] - width, cells.shape[dim], axis=dim)
        cells = jnp.concatenate(
            [
                lax.ppermute(tail, axis, [(i, (i + 1) % count) for i in range(ends)]),
                cells,
                lax.ppermute(head, axis, [((i + 1) % count, i) for i in range(ends)]),
            ],
            axis=dim,
        )
    return cells


def statistics(height, backscatter, grazing, weight):
    return [
        weight,
        weight * height,
        weight * height * height,
        weight * backscatter,
        weight * backscatter * backscatter,
        weight * height * backscatter,
        weight * grazing,
        weight * grazing * grazing,
    ]


def tap_weights(position, ext_side, margin):
    offsets = jnp.arange(ext_side, dtype=jnp.int32)[None, :] - position[:, None]
    inside = (offsets >= 0) & (offsets <= 2 * margin)
    spots = jnp.arange(-margin, margin + 1).astype(jnp.float32)
    profile_sum = jnp.sum(jnp.exp(-0.5 * (spots / gauss_sigma) * (spots / gauss_sigma)))
    centred = (offsets - margin).astype(jnp.float32) / gauss_sigma
    return jnp.where(inside, jnp.exp(-0.5 * centred * centred) / profile_sum, 0.0)


def fold_rims(extended, which_dim, tile_side, margin):
    ext_side = tile_side + 2 * margin
    inside_part = lax.slice_in_dim(extended, 2 * margin, 2 * margin + tile_side, axis=which_dim)
    lower_rim = lax.slice_in_dim(extended, 0, margin, axis=which_dim)
    upper_rim = lax.slice_in_dim(extended, ext_side + margin, ext_side + 2 * margin, axis=which_dim)
    pad_before = [(0, 0), (0, 0), (0, 0)]
    pad_before[which_dim] = (0, tile_side - margin)
    pad_after = [(0, 0), (0, 0), (0, 0)]
    pad_after[which_dim] = (tile_side - margin, 0)
    return inside_part + jnp.pad(lower_rim, pad_before) + jnp.pad(upper_rim, pad_after)


def shards(
    beam_depth,
    backscatter,
    grazing,
    quality,
    beam_valid,
    beam_row,
    beam_col,
    tidal_zone,
    ping_tile,
    tide_offsets,
):
    tile_rows = lax.axis_size("ty")
    tile_cols = lax.axis_size("tx")
    devices = tile_rows * tile_cols
    ping_count, beam_count = beam_depth.shape
    capacity = 4 * ping_count // devices
    slot_total = devices * capacity
    tile_side = TILE
    margin = MARGIN
    ext_side = tile_side + 2 * margin
    zone_count = tide_offsets.shape[0]
    zone_match = tidal_zone[:, None] == jnp.arange(zone_count, dtype=jnp.int32)[None, :]
    offset = jnp.sum(jnp.where(zone_match, tide_offsets[None, :], 0.0), axis=1)
    height = offset[:, None] - beam_depth
    weight = quality * beam_valid.astype(jnp.float32)
    cell_index = ((beam_row + margin) * ext_side + beam_col + margin).astype(jnp.float32)[None]
    same_tile = ping_tile[:, None] == ping_tile[None, :]
    earlier = jnp.arange(ping_count)[None, :] < jnp.arange(ping_count)[:, None]
    slot_rank = jnp.sum((same_tile & earlier).astype(jnp.int32), axis=1)
    slot_index = ping_tile * capacity + slot_rank
    slot_match = (jnp.arange(slot_total, dtype=jnp.int32)[:, None] == slot_index[None, :]).astype(
        jnp.float32
    )
    payload = jnp.stack([height, backscatter, grazing, weight], 0)
    packed = jnp.einsum("sp,fpb->fsb", slot_match, payload, precision=lax.Precision.HIGHEST)
    placed = jnp.einsum(
        "sp,fpb->fsb", slot_match, cell_index, precision=lax.Precision.HIGHEST
    ).astype(jnp.int32)
    arrived, landing_cell = (
        lax.all_to_all(packed, ("ty", "tx"), split_axis=1, concat_axis=1, tiled=True),
        lax.all_to_all(placed, ("ty", "tx"), split_axis=1, concat_axis=1, tiled=True),
    )
    values = jnp.stack(statistics(arrived[0], arrived[1], arrived[2], arrived[3]), 0)
    channel_count = values.shape[0]
    block_slots = math.gcd(slot_total, max(1, 8192 // beam_count))
    turns = slot_total // block_slots
    block_len = block_slots * beam_count
    value_blocks = values.reshape(channel_count, turns, block_len)
    cell_blocks = landing_cell.reshape(turns, block_len)

    def deposit_block(turn, total):
        block_values = lax.dynamic_index_in_dim(value_blocks, turn, 1, keepdims=False)
        block_cells = lax.dynamic_index_in_dim(cell_blocks, turn, 0, keepdims=False)
        row_weights = tap_weights(block_cells // ext_side - margin, ext_side, margin)
        col_weights = tap_weights(block_cells % ext_side - margin, ext_side, margin)
        left_side = block_values[:, :, None] * row_weights[None]
        return total + jnp.einsum(
            "cnr,nk->crk", left_side, col_weights, precision=lax.Precision.HIGHEST
        )

    deposit_grid = lax.fori_loop(
        0, turns, deposit_block, jnp.zeros((channel_count, ext_side, ext_side), jnp.float32)
    )
    extended = extended_2(deposit_grid, (("ty", 1), ("tx", 2)), margin)
    summed = fold_rims(fold_rims(extended, 1, tile_side, margin), 2, tile_side, margin)
    return summed / (1.0 + summed[0])[None]


def solution(mesh):
    placed = (
        P(("ty", "tx"), None),
        P(("ty", "tx"), None),
        P(("ty", "tx"), None),
        P(("ty", "tx"), None),
        P(("ty", "tx"), None),
        P(("ty", "tx"), None),
        P(("ty", "tx"), None),
        P(("ty", "tx")),
        P(("ty", "tx")),
        P(),
    )
    return jax.shard_map(
        shards, mesh=mesh, in_specs=placed, out_specs=P(None, "ty", "tx"), check_vma=False
    )
```

profile of v0, /device:TPU:0, one launch (start us, length us, event | category | flops | bytes accessed | tf_op | source)
XLA Modules:
  0.0 524.4 jit_solution(6398440578930417857)
XLA Ops:
  4.1 11.2 %all-to-all-start.1 = ((s32[1,256,512]{2,0,1:T(1,128)}), s32[1,256,512]{2,0,1:T(1,128)S(1)}, u32[]{:S(2)}, u32[]{:S(2)}) async-start(s32[1,256,512]{2,0,1:T(1,128)} %copy.25), calls=%async_computation.1 | async-start | bytes 1048576 | tf_op jit(solution)/shard_map/all_to_all | solution.py:107
  16.7 2.0 copy.24
  18.7 10.2 %all-to-all-done.1 = s32[1,256,512]{2,0,1:T(1,128)S(1)} async-done(((s32[1,256,512]{2,0,1:T(1,128)}), s32[1,256,512]{2,0,1:T(1,128)S(1)}, u32[]{:S(2)}, u32[]{:S(2)}) %all-to-all-start.1) | async-done | bytes 524320 | tf_op jit(solution)/shard_map/all_to_all | solution.py:107
  28.9 4.8 all-to-all-start
  35.9 27.4 %all-to-all-done = f32[4,256,512]{2,0,1:T(4,128)S(1)} async-done(((f32[4,256,512]{2,0,1:T(4,128)}), f32[4,256,512]{2,0,1:T(4,128)S(1)}, u32[]{:S(2)}, u32[]{:S(2)}) %all-to-all-start) | async-done | bytes 2097184 | tf_op jit(solution)/shard_map/all_to_all | solution.py:106
  63.2 14.3 %multiply_reduce_fusion = (f32[256,512]{1,0:T(8,128)S(1)}, f32[256,512]{1,0:T(8,128)}, f32[256,512]{1,0:T(8,128)S(1)}, f32[256,512]{1,0:T(8,128)}, f32[256,512]{...) fusion(f32[4,256,512]{2,0,1:T(4,128)S(1)} %all-to-all-done), kind=kLoop, calls=%fused_computation.58 | loop fusion | flops 917504 | bytes 6291456 | tf_op jit(solution)/shard_map/mul | solution.py:41
  79.7 2.0 stack.47
  83.1 1.9 constant_dynamic-update-slice_fusion.6
  85.0 1.9 constant_dynamic-update-slice_fusion.5
  91.1 410.9 %while.17 = (s32[]{:T(128)}, f32[8,78,78]{2,1,0:T(8,128)S(1)}, f32[8,16,8192]{2,1,0:T(8,128)}, s32[16,8192]{1,0:T(8,128)}, s32[]{:T(128)}, /*index=5*/s32[]{:T(128)}) while((s32[]{:T(128)}, f32[8,78,78]{2,1,0:T(8,128)S(1)}, f32[8,16,8192]{2,1,0:T(8,128)}, s32[16,8192]{1,0:T(8,128)}, s32[]{:T(128)}, /*index=5*/s32[]{:T(128)}) %tuple.63), condition=%wide.region_4.5_spmd.clone, body=%wide.region_2.4_spmd.clone.sunk | while | flops 4804033536 | bytes 7156071 | solution.py:127
  93.9 1.6 divide_select_fusion.2
  95.6 1.8 constant_dynamic-slice_fusion.2
  97.5 19.2 %fusion.85 = f32[8,78,78]{2,1,0:T(8,128)S(1)} fusion(s32[8192]{0:T(1024)S(1)} %get-tuple-element.237, f32[]{:T(128)} %exponential_reduce_fusion.2, f32[8192,78]{0,1:T(8,128)S(1)} %divide_select_fusion.2, f32[8,8192]{1,0:T(8,128)S(1)} %bitcast.35, f32[8,78,78]{2,1,0:T(8,128)S(1)} %get-tuple-element.246, pred[]{:T(512)S(6)} %compare.29), kind=kOutput, calls=%fused_computation.30.clone.1 | convolution fusion | flops 4796890112 | bytes 3240197 | tf_op jit(solution)/shard_map/while/body/eval_jaxpr/cnr,nk->crk/dot_general | solution.py:123
  119.6 1.6 divide_select_fusion.2
  121.3 1.8 constant_dynamic-slice_fusion.2
  123.2 19.2 %fusion.85 = f32[8,78,78]{2,1,0:T(8,128)S(1)} fusion(s32[8192]{0:T(1024)S(1)} %get-tuple-element.237, f32[]{:T(128)} %exponential_reduce_fusion.2, f32[8192,78]{0,1:T(8,128)S(1)} %divide_select_fusion.2, f32[8,8192]{1,0:T(8,128)S(1)} %bitcast.35, f32[8,78,78]{2,1,0:T(8,128)S(1)} %get-tuple-element.246, pred[]{:T(512)S(6)} %compare.29), kind=kOutput, calls=%fused_computation.30.clone.1 | convolution fusion | flops 4796890112 | bytes 3240197 | tf_op jit(solution)/shard_map/while/body/eval_jaxpr/cnr,nk->crk/dot_general | solution.py:123
  146.9 1.8 constant_dynamic-slice_fusion.2
  148.9 19.2 %fusion.85 = f32[8,78,78]{2,1,0:T(8,128)S(1)} fusion(s32[8192]{0:T(1024)S(1)} %get-tuple-element.237, f32[]{:T(128)} %exponential_reduce_fusion.2, f32[8192,78]{0,1:T(8,128)S(1)} %divide_select_fusion.2, f32[8,8192]{1,0:T(8,128)S(1)} %bitcast.35, f32[8,78,78]{2,1,0:T(8,128)S(1)} %get-tuple-element.246, pred[]{:T(512)S(6)} %compare.29), kind=kOutput, calls=%fused_computation.30.clone.1 | convolution fusion | flops 4796890112 | bytes 3240197 | tf_op jit(solution)/shard_map/while/body/eval_jaxpr/cnr,nk->crk/dot_general | solution.py:123
  172.6 1.8 constant_dynamic-slice_fusion.2
  174.6 19.2 %fusion.85 = f32[8,78,78]{2,1,0:T(8,128)S(1)} fusion(s32[8192]{0:T(1024)S(1)} %get-tuple-element.237, f32[]{:T(128)} %exponential_reduce_fusion.2, f32[8192,78]{0,1:T(8,128)S(1)} %divide_select_fusion.2, f32[8,8192]{1,0:T(8,128)S(1)} %bitcast.35, f32[8,78,78]{2,1,0:T(8,128)S(1)} %get-tuple-element.246, pred[]{:T(512)S(6)} %compare.29), kind=kOutput, calls=%fused_computation.30.clone.1 | convolution fusion | flops 4796890112 | bytes 3240197 | tf_op jit(solution)/shard_map/while/body/eval_jaxpr/cnr,nk->crk/dot_general | solution.py:123
  198.3 1.8 constant_dynamic-slice_fusion.2
  200.3 19.2 %fusion.85 = f32[8,78,78]{2,1,0:T(8,128)S(1)} fusion(s32[8192]{0:T(1024)S(1)} %get-tuple-element.237, f32[]{:T(128)} %exponential_reduce_fusion.2, f32[8192,78]{0,1:T(8,128)S(1)} %divide_select_fusion.2, f32[8,8192]{1,0:T(8,128)S(1)} %bitcast.35, f32[8,78,78]{2,1,0:T(8,128)S(1)} %get-tuple-element.246, pred[]{:T(512)S(6)} %compare.29), kind=kOutput, calls=%fused_computation.30.clone.1 | convolution fusion | flops 4796890112 | bytes 3240197 | tf_op jit(solution)/shard_map/while/body/eval_jaxpr/cnr,nk->crk/dot_general | solution.py:123
  224.0 1.8 constant_dynamic-slice_fusion.2
  226.0 19.2 %fusion.85 = f32[8,78,78]{2,1,0:T(8,128)S(1)} fusion(s32[8192]{0:T(1024)S(1)} %get-tuple-element.237, f32[]{:T(128)} %exponential_reduce_fusion.2, f32[8192,78]{0,1:T(8,128)S(1)} %divide_select_fusion.2, f32[8,8192]{1,0:T(8,128)S(1)} %bitcast.35, f32[8,78,78]{2,1,0:T(8,128)S(1)} %get-tuple-element.246, pred[]{:T(512)S(6)} %compare.29), kind=kOutput, calls=%fused_computation.30.clone.1 | convolution fusion | flops 4796890112 | bytes 3240197 | tf_op jit(solution)/shard_map/while/body/eval_jaxpr/cnr,nk->crk/dot_general | solution.py:123
  249.7 1.8 constant_dynamic-slice_fusion.2
  251.7 19.2 %fusion.85 = f32[8,78,78]{2,1,0:T(8,128)S(1)} fusion(s32[8192]{0:T(1024)S(1)} %get-tuple-element.237, f32[]{:T(128)} %exponential_reduce_fusion.2, f32[8192,78]{0,1:T(8,128)S(1)} %divide_select_fusion.2, f32[8,8192]{1,0:T(8,128)S(1)} %bitcast.35, f32[8,78,78]{2,1,0:T(8,128)S(1)} %get-tuple-element.246, pred[]{:T(512)S(6)} %compare.29), kind=kOutput, calls=%fused_computation.30.clone.1 | convolution fusion | flops 4796890112 | bytes 3240197 | tf_op jit(solution)/shard_map/while/body/eval_jaxpr/cnr,nk->crk/dot_general | solution.py:123
  275.4 1.8 constant_dynamic-slice_fusion.2
  277.3 19.2 %fusion.85 = f32[8,78,78]{2,1,0:T(8,128)S(1)} fusion(s32[8192]{0:T(1024)S(1)} %get-tuple-element.237, f32[]{:T(128)} %exponential_reduce_fusion.2, f32[8192,78]{0,1:T(8,128)S(1)} %divide_select_fusion.2, f32[8,8192]{1,0:T(8,128)S(1)} %bitcast.35, f32[8,78,78]{2,1,0:T(8,128)S(1)} %get-tuple-element.246, pred[]{:T(512)S(6)} %compare.29), kind=kOutput, calls=%fused_computation.30.clone.1 | convolution fusion | flops 4796890112 | bytes 3240197 | tf_op jit(solution)/shard_map/while/body/eval_jaxpr/cnr,nk->crk/dot_general | solution.py:123
  301.1 1.8 constant_dynamic-slice_fusion.2
  303.0 19.2 %fusion.85 = f32[8,78,78]{2,1,0:T(8,128)S(1)} fusion(s32[8192]{0:T(1024)S(1)} %get-tuple-element.237, f32[]{:T(128)} %exponential_reduce_fusion.2, f32[8192,78]{0,1:T(8,128)S(1)} %divide_select_fusion.2, f32[8,8192]{1,0:T(8,128)S(1)} %bitcast.35, f32[8,78,78]{2,1,0:T(8,128)S(1)} %get-tuple-element.246, pred[]{:T(512)S(6)} %compare.29), kind=kOutput, calls=%fused_computation.30.clone.1 | convolution fusion | flops 4796890112 | bytes 3240197 | tf_op jit(solution)/shard_map/while/body/eval_jaxpr/cnr,nk->crk/dot_general | solution.py:123
  326.7 1.8 constant_dynamic-slice_fusion.2
  328.7 19.2 %fusion.85 = f32[8,78,78]{2,1,0:T(8,128)S(1)} fusion(s32[8192]{0:T(1024)S(1)} %get-tuple-element.237, f32[]{:T(128)} %exponential_reduce_fusion.2, f32[8192,78]{0,1:T(8,128)S(1)} %divide_select_fusion.2, f32[8,8192]{1,0:T(8,128)S(1)} %bitcast.35, f32[8,78,78]{2,1,0:T(8,128)S(1)} %get-tuple-element.246, pred[]{:T(512)S(6)} %compare.29), kind=kOutput, calls=%fused_computation.30.clone.1 | convolution fusion | flops 4796890112 | bytes 3240197 | tf_op jit(solution)/shard_map/while/body/eval_jaxpr/cnr,nk->crk/dot_general | solution.py:123
  352.4 1.8 constant_dynamic-slice_fusion.2
  354.4 19.2 %fusion.85 = f32[8,78,78]{2,1,0:T(8,128)S(1)} fusion(s32[8192]{0:T(1024)S(1)} %get-tuple-element.237, f32[]{:T(128)} %exponential_reduce_fusion.2, f32[8192,78]{0,1:T(8,128)S(1)} %divide_select_fusion.2, f32[8,8192]{1,0:T(8,128)S(1)} %bitcast.35, f32[8,78,78]{2,1,0:T(8,128)S(1)} %get-tuple-element.246, pred[]{:T(512)S(6)} %compare.29), kind=kOutput, calls=%fused_computation.30.clone.1 | convolution fusion | flops 4796890112 | bytes 3240197 | tf_op jit(solution)/shard_map/while/body/eval_jaxpr/cnr,nk->crk/dot_general | solution.py:123
  378.1 1.8 constant_dynamic-slice_fusion.2
  380.1 19.2 %fusion.85 = f32[8,78,78]{2,1,0:T(8,128)S(1)} fusion(s32[8192]{0:T(1024)S(1)} %get-tuple-element.237, f32[]{:T(128)} %exponential_reduce_fusion.2, f32[8192,78]{0,1:T(8,128)S(1)} %divide_select_fusion.2, f32[8,8192]{1,0:T(8,128)S(1)} %bitcast.35, f32[8,78,78]{2,1,0:T(8,128)S(1)} %get-tuple-element.246, pred[]{:T(512)S(6)} %compare.29), kind=kOutput, calls=%fused_computation.30.clone.1 | convolution fusion | flops 4796890112 | bytes 3240197 | tf_op jit(solution)/shard_map/while/body/eval_jaxpr/cnr,nk->crk/dot_general | solution.py:123
  403.8 1.8 constant_dynamic-slice_fusion.2
  405.8 19.2 %fusion.85 = f32[8,78,78]{2,1,0:T(8,128)S(1)} fusion(s32[8192]{0:T(1024)S(1)} %get-tuple-element.237, f32[]{:T(128)} %exponential_reduce_fusion.2, f32[8192,78]{0,1:T(8,128)S(1)} %divide_select_fusion.2, f32[8,8192]{1,0:T(8,128)S(1)} %bitcast.35, f32[8,78,78]{2,1,0:T(8,128)S(1)} %get-tuple-element.246, pred[]{:T(512)S(6)} %compare.29), kind=kOutput, calls=%fused_computation.30.clone.1 | convolution fusion | flops 4796890112 | bytes 3240197 | tf_op jit(solution)/shard_map/while/body/eval_jaxpr/cnr,nk->crk/dot_general | solution.py:123
  429.5 1.8 constant_dynamic-slice_fusion.2
  431.4 19.2 %fusion.85 = f32[8,78,78]{2,1,0:T(8,128)S(1)} fusion(s32[8192]{0:T(1024)S(1)} %get-tuple-element.237, f32[]{:T(128)} %exponential_reduce_fusion.2, f32[8192,78]{0,1:T(8,128)S(1)} %divide_select_fusion.2, f32[8,8192]{1,0:T(8,128)S(1)} %bitcast.35, f32[8,78,78]{2,1,0:T(8,128)S(1)} %get-tuple-element.246, pred[]{:T(512)S(6)} %compare.29), kind=kOutput, calls=%fused_computation.30.clone.1 | convolution fusion | flops 4796890112 | bytes 3240197 | tf_op jit(solution)/shard_map/while/body/eval_jaxpr/cnr,nk->crk/dot_general | solution.py:123
  455.2 1.8 constant_dynamic-slice_fusion.2
  457.1 19.2 %fusion.85 = f32[8,78,78]{2,1,0:T(8,128)S(1)} fusion(s32[8192]{0:T(1024)S(1)} %get-tuple-element.237, f32[]{:T(128)} %exponential_reduce_fusion.2, f32[8192,78]{0,1:T(8,128)S(1)} %divide_select_fusion.2, f32[8,8192]{1,0:T(8,128)S(1)} %bitcast.35, f32[8,78,78]{2,1,0:T(8,128)S(1)} %get-tuple-element.246, pred[]{:T(512)S(6)} %compare.29), kind=kOutput, calls=%fused_computation.30.clone.1 | convolution fusion | flops 4796890112 | bytes 3240197 | tf_op jit(solution)/shard_map/while/body/eval_jaxpr/cnr,nk->crk/dot_general | solution.py:123
  480.8 1.8 constant_dynamic-slice_fusion.2
  482.8 19.2 %fusion.85 = f32[8,78,78]{2,1,0:T(8,128)S(1)} fusion(s32[8192]{0:T(1024)S(1)} %get-tuple-element.237, f32[]{:T(128)} %exponential_reduce_fusion.2, f32[8192,78]{0,1:T(8,128)S(1)} %divide_select_fusion.2, f32[8,8192]{1,0:T(8,128)S(1)} %bitcast.35, f32[8,78,78]{2,1,0:T(8,128)S(1)} %get-tuple-element.246, pred[]{:T(512)S(6)} %compare.29), kind=kOutput, calls=%fused_computation.30.clone.1 | convolution fusion | flops 4796890112 | bytes 3240197 | tf_op jit(solution)/shard_map/while/body/eval_jaxpr/cnr,nk->crk/dot_general | solution.py:123
  504.7 3.0 collective-permute-done.1
  507.9 2.6 collective-permute-start.2
  511.8 6.4 %collective-permute-done.2 = f32[8,92,7]{2,1,0:T(8,128)S(1)} collective-permute-done((f32[8,92,7]{2,1,0:T(8,128)S(1)}, f32[8,92,7]{2,1,0:T(8,128)S(1)}, u32[]{:S(2)}, u32[]{:S(2)}) %collective-permute-start.2) | collective-permute-done | bytes 20640 | tf_op jit(solution)/shard_map/ppermute | solution.py:23
  518.2 4.7 collective-permute-done.3
  (154 shorter events, 91.5 us)
Async XLA Ops:
  0.0 15.3 %copy-start.11 = (s32[64]{0:T(128)S(1)}, s32[64]{0:T(128)}, u32[]{:S(2)}) copy-start(s32[64]{0:T(128)} %param.19) | copy-start | bytes 772
  0.0 15.3 %copy-start.10 = (f32[64]{0:T(128)S(1)}, f32[64]{0:T(128)}, u32[]{:S(2)}) copy-start(f32[64]{0:T(128)} %param.21) | copy-start | bytes 772
  0.0 15.5 %copy-start.8 = (f32[64,512]{1,0:T(8,128)S(1)}, f32[64,512]{1,0:T(8,128)}, u32[]{:S(2)}) copy-start(f32[64,512]{1,0:T(8,128)} %param.12) | copy-start | bytes 393220
  0.0 15.5 %copy-start.6 = (f32[64,512]{1,0:T(8,128)S(1)}, f32[64,512]{1,0:T(8,128)}, u32[]{:S(2)}) copy-start(f32[64,512]{1,0:T(8,128)} %param.15) | copy-start | bytes 393220
  0.0 15.5 %copy-start.7 = (s32[64,512]{1,0:T(8,128)S(1)}, s32[64,512]{1,0:T(8,128)}, u32[]{:S(2)}) copy-start(s32[64,512]{1,0:T(8,128)} %param.16) | copy-start | bytes 393220
  0.0 15.6 %copy-start.5 = (f32[64,512]{1,0:T(8,128)S(1)}, f32[64,512]{1,0:T(8,128)}, u32[]{:S(2)}) copy-start(f32[64,512]{1,0:T(8,128)} %param.13) | copy-start | bytes 393220
  0.0 15.6 %copy-start.4 = (f32[64,512]{1,0:T(8,128)S(1)}, f32[64,512]{1,0:T(8,128)}, u32[]{:S(2)}) copy-start(f32[64,512]{1,0:T(8,128)} %param.14) | copy-start | bytes 393220
  4.1 24.8 %all-to-all-start.1 = ((s32[1,256,512]{2,0,1:T(1,128)}), s32[1,256,512]{2,0,1:T(1,128)S(1)}, u32[]{:S(2)}, u32[]{:S(2)}) async-start(s32[1,256,512]{2,0,1:T(1,128)} %copy.25), calls=%async_computation.1 | async-start | bytes 1048576 | tf_op jit(solution)/shard_map/all_to_all | solution.py:107
  28.9 34.4 %all-to-all-start = ((f32[4,256,512]{2,0,1:T(4,128)}), f32[4,256,512]{2,0,1:T(4,128)S(1)}, u32[]{:S(2)}, u32[]{:S(2)}) async-start(f32[4,256,512]{2,0,1:T(4,128)} %copy.24), calls=%async_computation | async-start | bytes 4194304 | tf_op jit(solution)/shard_map/all_to_all | solution.py:106
  77.6 5.0 copy-start.3
  77.6 5.1 copy-start.2
  78.8 4.0 copy-start.1
  79.7 3.2 copy-start
  502.0 21.2 %copy-start.9 = (pred[64]{0:T(512)(128)(4,1)S(1)}, pred[64]{0:T(512)(128)(4,1)}, u32[]{:S(2)}) copy-start(pred[64]{0:T(512)(128)(4,1)} %constant.166.clone.1) | copy-start | bytes 196
  502.1 2.6 collective-permute-start
  503.4 4.3 collective-permute-start.1
  507.9 10.3 %collective-permute-start.2 = (f32[8,92,7]{2,1,0:T(8,128)S(1)}, f32[8,92,7]{2,1,0:T(8,128)S(1)}, u32[]{:S(2)}, u32[]{:S(2)}) collective-permute-start(f32[8,92,7]{2,1,0:T(8,128)S(1)} %get-tuple-element.200), channel_id=1, source_target_pairs={{0,1},{1,2},{2,3},{3,4},{4,5},{5,6},{6,7},{7,8},{8,9},{9,10},{10,1... | collective-permute-start | bytes 61832 | tf_op jit(solution)/shard_map/ppermute | solution.py:23
  510.5 12.5 %collective-permute-start.3 = (f32[8,92,7]{2,1,0:T(8,128)S(1)}, f32[8,92,7]{2,1,0:T(8,128)S(1)}, u32[]{:S(2)}, u32[]{:S(2)}) collective-permute-start(f32[8,92,7]{2,1,0:T(8,128)S(1)} %get-tuple-element.201), channel_id=1, source_target_pairs={{1,0},{2,1},{3,2},{4,3},{5,4},{6,5},{7,6},{8,7},{9,8},{10,9},{11,1... | collective-permute-start | bytes 61832 | tf_op jit(solution)/shard_map/ppermute | solution.py:25
where the time goes:
time: 530 us; the launch traced here: 524 us
  matrix products  310 us (58%)
  other arithmetic  90.3 us (17%)
  waiting for transfers between devices  51.7 us (10%)
  local copies, waits for them, and re-layouts  49 us (9%)
  starting transfers between devices  22.5 us (4%)
    dot_general x16, matrix products, deposit_block(): jnp.einsum('cnr,nk->crk', left_side, col_weights, precision=lax.Precision...  307 us
    dynamic_slice x32, local copies, waits for them, and re-layouts, deposit_block(): lax.dynamic_index_in_dim(value_blocks, turn, 1, keepdims=False)  31.3 us
    all_to_all x1, waiting for transfers between devices, shards(): lax.all_to_all(packed, ('ty', 'tx'), split_axis=1, concat_axis=1, tiled=T...  27.4 us
    select_n x16, other arithmetic, tap_weights(): jnp.where(inside, jnp.exp(-0.5 * centred * centred) / profile_sum, 0.0)  26.4 us
    div x16, other arithmetic, deposit_block(): block_cells // ext_side - margin  17.7 us
    ne x16, other arithmetic, deposit_block(): block_cells // ext_side - margin  17.7 us
    mul x1, other arithmetic, statistics(): weight * grazing * grazing  14.3 us
    all_to_all x1, starting transfers between devices, shards(): lax.all_to_all(placed, ('ty', 'tx'), split_axis=1, concat_axis=1, tiled=T...  11.2 us
  transfers between devices with their start and end apart: 6, of which 5 were waited for; matrix products, arithmetic and copies ran while one was open for 1% of the time, Pallas kernels for 0%

commit v1 on v0

v1 whole, which is shorter than its diff:
```python
import functools
import math

import jax
import jax.numpy as jnp
from jax import lax
from jax.experimental import pallas as pl
from jax.experimental.pallas import tpu as pltpu
from jax.sharding import PartitionSpec as P

F32 = jnp.float32
BF16 = jnp.bfloat16
BEAMS = 512
CHANNELS = 8
MARGIN = 7
TILE = 64
FIELDS = 5
LANES = 128
GROUPS = BEAMS // LANES
RANKS = 2
BATCH = 8
SIGMA = 2.5
VMEM = pltpu.CompilerParams(vmem_limit_bytes=40 * 2**20)

_profile = [math.exp(-j * j / (2 * SIGMA * SIGMA)) for j in range(-MARGIN, MARGIN + 1)]
TAPS = [value / sum(_profile) for value in _profile]


def vmem():
    return pl.BlockSpec(memory_space=pltpu.VMEM)


def smem():
    return pl.BlockSpec(memory_space=pltpu.SMEM)


def pack_kernel(tile, zone, tide, depth, back, graz, quality, valid, row, col, out, seen):
    pings = depth.shape[0]
    slots = out.shape[0]

    def clear(i, _):
        seen[i] = 0
        return 0

    lax.fori_loop(0, slots // RANKS, clear, 0, unroll=8)

    def empty(i, _):
        out[i, FIELDS - 1] = jnp.full((GROUPS, LANES), -1.0, F32)
        return 0

    lax.fori_loop(0, slots, empty, 0, unroll=8)

    def place(p, _):
        target = tile[p]
        rank = seen[target]
        seen[target] = rank + 1
        slot = target * RANKS + rank
        offset = tide[zone[p]]
        here = pl.ds(p, 1)
        fields = (
            offset - depth[here, :],
            back[here, :],
            graz[here, :],
            quality[here, :] * valid[here, :].astype(F32),
            (row[here, :] * TILE + col[here, :]).astype(F32),
        )
        for f, values in enumerate(fields):
            for j in range(GROUPS):
                out[slot, f, pl.ds(j, 1), :] = values[:, j * LANES : (j + 1) * LANES]
        return 0

    lax.fori_loop(0, pings, place, 0, unroll=4)


def both(rows):
    return jnp.concatenate([rows, rows], 0).astype(BF16)


def factors(x, slot, spots):
    sub = lax.broadcasted_iota(jnp.int32, (8, LANES), 0)
    zero = jnp.zeros((16, LANES), BF16)
    one = jnp.ones((16, LANES), BF16)
    left, right = [], []
    for j in range(GROUPS):
        height, back, graz, weight, cell = (
            jnp.broadcast_to(x[slot, f, pl.ds(j, 1), :], (8, LANES)) for f in range(FIELDS)
        )
        first = jnp.where(
            (sub == 1) | (sub == 2) | (sub == 5),
            height,
            jnp.where((sub == 3) | (sub == 4), back, jnp.where(sub >= 6, graz, 1.0)),
        )
        second = jnp.where(
            sub == 2,
            height,
            jnp.where((sub == 4) | (sub == 5), back, jnp.where(sub == 7, graz, 1.0)),
        )
        stats = weight * first * second
        high = stats.astype(BF16).astype(F32)
        halves = jnp.concatenate([high, stats - high], 0).astype(BF16)
        coarse = jnp.floor(cell * (1.0 / 256.0))
        fine = both(cell - 256.0 * coarse)
        coarse = both(coarse)
        left.append(
            jnp.concatenate(
                [jnp.where(coarse == jnp.asarray(r, BF16), halves, zero) for r in range(16)], 0
            )
        )
        right.append(jnp.concatenate([jnp.where(fine == s, one, zero) for s in spots], 0))
    return jnp.concatenate(left, 1), jnp.concatenate(right, 1)


def deposit_kernel(first_cell, x, out, low, high, acc, order):
    slots = x.shape[0]

    def note(s, carry):
        count, gap = carry
        filled = first_cell[s] >= 0
        order[count] = s
        return count + filled.astype(jnp.int32), jnp.where(filled, gap, s)

    count, gap = lax.fori_loop(0, slots, note, (jnp.int32(0), jnp.int32(0)), unroll=8)
    for u in range(BATCH):
        order[count + u] = gap

    acc[...] = jnp.zeros_like(acc)
    base = lax.broadcasted_iota(jnp.int32, (16, LANES), 0)
    spots = [(base + 16 * i).astype(F32).astype(BF16) for i in range(16)]

    def step(t, _):
        pairs = [factors(x, order[t * BATCH + u], spots) for u in range(BATCH)]
        left = jnp.concatenate([a for a, _ in pairs], 1)
        right = jnp.concatenate([b for _, b in pairs], 1)
        part = lax.dot_general(
            left, right, (((1,), (1,)), ((), ())), preferred_element_type=F32
        )
        acc[0] += part[:, :LANES]
        acc[1] += part[:, LANES:]
        return 0

    lax.fori_loop(0, (count + BATCH - 1) // BATCH, step, 0)
    for ch in range(CHANNELS):
        for half in range(2):
            rows = acc[half, pl.ds(ch, 16, stride=16), :] + acc[half, pl.ds(ch + 8, 16, stride=16), :]
            for q in range(2):
                out[ch, pl.ds(2 * half + q, 16, stride=4), 0:TILE] = rows[:, q * TILE : (q + 1) * TILE]
        low[ch] = out[ch, 0:8, 0:TILE]
        high[ch] = out[ch, TILE - 8 : TILE, 0:TILE]


def smoothed_rows(ext, ch):
    total = None
    for j in range(2 * MARGIN + 1):
        term = TAPS[j] * ext[ch, pl.ds(1 + j, TILE), :]
        total = term if total is None else total + term
    return total


def extend(ext, before, own, after):
    for ch in range(CHANNELS):
        ext[ch, 0:8, :] = before[ch]
        ext[ch, 8 : 8 + TILE, :] = own[ch, :, 0:TILE]
        ext[ch, 8 + TILE : 16 + TILE, :] = after[ch]


def rows_kernel(before, own, after, out, low, high, ext):
    extend(ext, before, own, after)
    for ch in range(CHANNELS):
        turned = smoothed_rows(ext, ch).T
        out[ch] = turned
        low[ch] = turned[0:8]
        high[ch] = turned[TILE - 8 : TILE]


def columns_kernel(before, own, after, out, ext):
    extend(ext, before, own, after)
    scale = None
    for ch in range(CHANNELS):
        total = smoothed_rows(ext, ch)
        if ch == 0:
            scale = 1.0 + total
        out[ch] = (total / scale).T


def shift(x, axis, step):
    count = lax.axis_size(axis)
    return lax.ppermute(
        x, axis, [(i, i + step) for i in range(count) if 0 <= i + step < count]
    )


def shards(depth, back, graz, quality, valid, row, col, zone, tile, tide):
    devices = lax.axis_size("ty") * lax.axis_size("tx")
    slots = devices * RANKS
    shape = jax.ShapeDtypeStruct
    packed = pl.pallas_call(
        pack_kernel,
        out_shape=shape((slots, FIELDS, GROUPS, LANES), F32),
        in_specs=[smem()] * 3 + [vmem()] * 7,
        out_specs=vmem(),
        scratch_shapes=[pltpu.SMEM((devices,), jnp.int32)],
        compiler_params=VMEM,
        name="pack",
    )(tile, zone, tide, depth, back, graz, quality, valid, row, col)
    arrived = lax.all_to_all(packed, ("ty", "tx"), split_axis=0, concat_axis=0, tiled=True)
    first_cell = arrived[:, FIELDS - 1, 0, 0].astype(jnp.int32)
    rim = shape((CHANNELS, 8, TILE), F32)
    deposit, low, high = pl.pallas_call(
        deposit_kernel,
        out_shape=(shape((CHANNELS, TILE, LANES), F32), rim, rim),
        in_specs=[smem(), vmem()],
        out_specs=(vmem(),) * 3,
        scratch_shapes=[
            pltpu.VMEM((2, 256, LANES), F32),
            pltpu.SMEM((slots + BATCH,), jnp.int32),
        ],
        compiler_params=VMEM,
        name="deposit",
    )(first_cell, arrived)
    rows, low, high = pl.pallas_call(
        rows_kernel,
        out_shape=(shape((CHANNELS, TILE, TILE), F32), rim, rim),
        in_specs=[vmem()] * 3,
        out_specs=(vmem(),) * 3,
        scratch_shapes=[pltpu.VMEM((CHANNELS, TILE + 16, TILE), F32)],
        compiler_params=VMEM,
        name="rows",
    )(shift(high, "ty", 1), deposit, shift(low, "ty", -1))
    return pl.pallas_call(
        columns_kernel,
        out_shape=shape((CHANNELS, TILE, TILE), F32),
        in_specs=[vmem()] * 3,
        out_specs=vmem(),
        scratch_shapes=[pltpu.VMEM((CHANNELS, TILE + 16, TILE), F32)],
        compiler_params=VMEM,
        name="columns",
    )(shift(high, "tx", 1), rows, shift(low, "tx", -1))


def solution(mesh):
    pings = P(("ty", "tx"))
    return jax.shard_map(
        shards,
        mesh=mesh,
        in_specs=(pings,) * 9 + (P(),),
        out_specs=P(None, "ty", "tx"),
        check_vma=False,
    )
```

time: 530 us -> 101 us (0.19)
  the two profiles are of different devices: /device:TPU:0 before, /device:TPU:24 now
where the time goes in v1:
time: 101 us; the launch traced here: 102 us
  blocking collectives  44.7 us (44%)
  starting transfers between devices  24.6 us (24%)
  Pallas kernels  11.2 us (11%)
  waiting for transfers between devices  8.59 us (9%)
  local copies, waits for them, and re-layouts  8.29 us (8%)
  other arithmetic  4.63 us (5%)
    all_to_all x1, blocking collectives, shards(): lax.all_to_all(packed, ('ty', 'tx'), split_axis=0, concat_axis=0, tiled=T...  44.7 us
    ppermute x4, starting transfers between devices, shift(): lax.ppermute(x, axis, [(i, i + step) for i in range(count) if 0 <= i + st...  24.6 us
    ppermute x4, waiting for transfers between devices, shift(): lax.ppermute(x, axis, [(i, i + step) for i in range(count) if 0 <= i + st...  8.59 us
    unnamed x20, local copies, waits for them, and re-layouts  8.29 us
    pallas_call x1, Pallas kernels, shards(): pl.pallas_call(deposit_kernel, out_shape=(shape((CHANNELS, TILE, LANES),...  8.26 us
    convert_element_type x1, other arithmetic, shards(): first_cell = arrived[:, FIELDS - 1, 0, 0].astype(jnp.int32)  4.63 us
  transfers between devices with their start and end apart: 4, of which 2 were waited for; matrix products, arithmetic and copies ran while one was open for 0% of the time, Pallas kernels for 0%

profile of v1, /device:TPU:24, one launch (start us, length us, event | category | flops | bytes accessed | tf_op | source)
XLA Modules:
  0.0 102.1 jit_solution(4192263416356796392)
XLA Ops:
  0.0 0.0 copy-start
  0.0 0.9 copy-done
  0.9 0.0 copy-start.1
  0.9 0.9 copy-done.1
  1.8 0.0 copy-start.2
  1.8 0.9 copy-done.2
  2.7 0.0 copy-start.3
  2.7 0.9 copy-done.3
  3.6 0.0 copy-start.4
  3.6 0.9 copy-done.4
  4.5 0.0 copy-start.5
  4.5 0.9 copy-done.5
  5.4 0.0 copy-start.6
  5.4 0.9 copy-done.6
  6.3 0.0 copy-start.7
  6.3 0.7 copy-done.7
  7.0 0.0 copy-start.8
  7.0 0.7 copy-done.8
  7.6 0.0 copy-start.9
  7.6 0.7 copy-done.9
  8.3 1.6 %pack.1 = f32[256,5,4,128]{3,2,1,0:T(4,128)S(1)} custom-call(s32[64]{0:T(128)S(1)} %copy-done.7, s32[64]{0:T(128)S(1)} %copy-done.8, f32[64]{0:T(128)S(1)} %copy-done.9, f32[64,512]{1,0:T(8,128)S(1)} %copy-done, f32[64,512]{1,0:T(8,128)S(1)} %copy-done.1, f32[64,512]{1,0:T(8,128)S(1)} %copy-done.2, f32[64,512]{1,0:T(8,128)S(1)} %copy-done.3, ...), custom_call_target="tpu_custom_call" | custom-call | tf_op jit(solution)/shard_map/pack/pallas_call | solution.py:196
  9.9 44.7 %all_to_all.5.x = f32[256,5,4,128]{3,2,1,0:T(4,128)S(1)} all-to-all(f32[256,5,4,128]{3,2,1,0:T(4,128)S(1)} %pack.1), channel_id=1, replica_groups=mesh['ty'=8,'tx'=16] {'ty','tx'}, dimensions={0} | all-to-all | bytes 5242880 | tf_op jit(solution)/shard_map/all_to_all | solution.py:205
  54.6 4.6 %fusion.first_cell = s32[256]{0:T(256)S(1)} fusion(f32[256,5,4,128]{3,2,1,0:T(4,128)S(1)} %all_to_all.5.x), kind=kLoop, calls=%fused_computation.1 | loop fusion | flops 256 | bytes 2048 | tf_op jit(solution)/shard_map/convert_element_type | solution.py:206
  59.3 8.3 %deposit.1 = (f32[8,64,128]{2,1,0:T(8,128)S(1)}, f32[8,8,64]{2,1,0:T(8,128)S(1)}, f32[8,8,64]{2,1,0:T(8,128)S(1)}) custom-call(s32[256]{0:T(256)S(1)} %fusion.first_cell, f32[256,5,4,128]{3,2,1,0:T(4,128)S(1)} %all_to_all.5.x), custom_call_target="tpu_custom_call" | custom-call | tf_op jit(solution)/shard_map/deposit/pallas_call | solution.py:208
  67.5 1.3 %collective-permute-start = (f32[8,8,64]{2,1,0:T(8,128)S(1)}, f32[8,8,64]{2,1,0:T(8,128)S(1)}, u32[]{:S(2)}, u32[]{:S(2)}) collective-permute-start(f32[8,8,64]{2,1,0:T(8,128)S(1)} %get-tuple-element.11), channel_id=1, source_target_pairs={{0,16},{16,32},{32,48},{48,64},{64,80},{80,96},{96,112},{1,17},{17... | collective-permute-start | bytes 49160 | tf_op jit(solution)/shard_map/ppermute | solution.py:187
  68.8 1.3 %collective-permute-start.1 = (f32[8,8,64]{2,1,0:T(8,128)S(1)}, f32[8,8,64]{2,1,0:T(8,128)S(1)}, u32[]{:S(2)}, u32[]{:S(2)}) collective-permute-start(f32[8,8,64]{2,1,0:T(8,128)S(1)} %get-tuple-element.13), channel_id=1, source_target_pairs={{16,0},{32,16},{48,32},{64,48},{80,64},{96,80},{112,96},{17,1},{33... | collective-permute-start | bytes 49160 | tf_op jit(solution)/shard_map/ppermute | solution.py:187
  70.1 0.0 collective-permute-done.before
  70.1 2.6 %collective-permute-done.1.after = f32[8,8,64]{2,1,0:T(8,128)S(1)} collective-permute-done((f32[8,8,64]{2,1,0:T(8,128)S(1)}, f32[8,8,64]{2,1,0:T(8,128)S(1)}, u32[]{:S(2)}, u32[]{:S(2)}) %collective-permute-start.1) | collective-permute-done | bytes 16416 | tf_op jit(solution)/shard_map/ppermute | solution.py:187
  72.7 0.3 rows.1
  73.1 20.1 %collective-permute-start.2 = (f32[8,8,64]{2,1,0:T(8,128)S(1)}, f32[8,8,64]{2,1,0:T(8,128)S(1)}, u32[]{:S(2)}, u32[]{:S(2)}) collective-permute-start(f32[8,8,64]{2,1,0:T(8,128)S(1)} %get-tuple-element.14), channel_id=1, source_target_pairs={{0,1},{1,2},{2,3},{3,4},{4,5},{5,6},{6,7},{7,8},{8,9},{9,10},{10,1... | collective-permute-start | bytes 49160 | tf_op jit(solution)/shard_map/ppermute | solution.py:187
  93.1 1.9 %collective-permute-start.3 = (f32[8,8,64]{2,1,0:T(8,128)S(1)}, f32[8,8,64]{2,1,0:T(8,128)S(1)}, u32[]{:S(2)}, u32[]{:S(2)}) collective-permute-start(f32[8,8,64]{2,1,0:T(8,128)S(1)} %get-tuple-element.16), channel_id=1, source_target_pairs={{1,0},{2,1},{3,2},{4,3},{5,4},{6,5},{7,6},{8,7},{9,8},{10,9},{11,1... | collective-permute-start | bytes 49160 | tf_op jit(solution)/shard_map/ppermute | solution.py:187
  95.1 0.0 collective-permute-done.2.before
  95.1 6.0 %collective-permute-done.3.after = f32[8,8,64]{2,1,0:T(8,128)S(1)} collective-permute-done((f32[8,8,64]{2,1,0:T(8,128)S(1)}, f32[8,8,64]{2,1,0:T(8,128)S(1)}, u32[]{:S(2)}, u32[]{:S(2)}) %collective-permute-start.3) | collective-permute-done | bytes 16416 | tf_op jit(solution)/shard_map/ppermute | solution.py:187
  101.1 1.0 %columns.1 = f32[8,64,64]{2,1,0:T(8,128)} custom-call(f32[8,8,64]{2,1,0:T(8,128)S(1)} %collective-permute-done.2.before, f32[8,64,64]{2,1,0:T(8,128)S(1)} %get-tuple-element.15.own, f32[8,8,64]{2,1,0:T(8,128)S(1)} %collective-permute-done.3.after), custom_call_target="tpu_custom_call" | custom-call | tf_op jit(solution)/shard_map/columns/pallas_call | solution.py:229
Async XLA Ops:
  0.0 0.9 copy-start
  0.9 0.9 copy-start.1
  1.8 0.9 copy-start.2
  2.7 0.9 copy-start.3
  3.6 0.9 copy-start.4
  4.5 0.9 copy-start.5
  5.4 0.9 copy-start.6
  6.3 0.7 copy-start.7
  7.0 0.7 copy-start.8
  7.6 0.7 copy-start.9
  67.5 2.6 %collective-permute-start = (f32[8,8,64]{2,1,0:T(8,128)S(1)}, f32[8,8,64]{2,1,0:T(8,128)S(1)}, u32[]{:S(2)}, u32[]{:S(2)}) collective-permute-start(f32[8,8,64]{2,1,0:T(8,128)S(1)} %get-tuple-element.11), channel_id=1, source_target_pairs={{0,16},{16,32},{32,48},{48,64},{64,80},{80,96},{96,112},{1,17},{17... | collective-permute-start | bytes 49160 | tf_op jit(solution)/shard_map/ppermute | solution.py:187
  68.8 3.9 %collective-permute-start.1 = (f32[8,8,64]{2,1,0:T(8,128)S(1)}, f32[8,8,64]{2,1,0:T(8,128)S(1)}, u32[]{:S(2)}, u32[]{:S(2)}) collective-permute-start(f32[8,8,64]{2,1,0:T(8,128)S(1)} %get-tuple-element.13), channel_id=1, source_target_pairs={{16,0},{32,16},{48,32},{64,48},{80,64},{96,80},{112,96},{17,1},{33... | collective-permute-start | bytes 49160 | tf_op jit(solution)/shard_map/ppermute | solution.py:187
  73.1 22.0 %collective-permute-start.2 = (f32[8,8,64]{2,1,0:T(8,128)S(1)}, f32[8,8,64]{2,1,0:T(8,128)S(1)}, u32[]{:S(2)}, u32[]{:S(2)}) collective-permute-start(f32[8,8,64]{2,1,0:T(8,128)S(1)} %get-tuple-element.14), channel_id=1, source_target_pairs={{0,1},{1,2},{2,3},{3,4},{4,5},{5,6},{6,7},{7,8},{8,9},{9,10},{10,1... | collective-permute-start | bytes 49160 | tf_op jit(solution)/shard_map/ppermute | solution.py:187
  93.1 7.9 %collective-permute-start.3 = (f32[8,8,64]{2,1,0:T(8,128)S(1)}, f32[8,8,64]{2,1,0:T(8,128)S(1)}, u32[]{:S(2)}, u32[]{:S(2)}) collective-permute-start(f32[8,8,64]{2,1,0:T(8,128)S(1)} %get-tuple-element.16), channel_id=1, source_target_pairs={{1,0},{2,1},{3,2},{4,3},{5,4},{6,5},{7,6},{8,7},{9,8},{10,9},{11,1... | collective-permute-start | bytes 49160 | tf_op jit(solution)/shard_map/ppermute | solution.py:187
